TPU v7x, 256 devices: a whole 4x4x8 slice. The times are simulated.
256 devices in a mesh: src: 8 (over y, core), tgt: 32 (over x, z).
Axes of the slice: x: 4, y: 4, z: 8, core: 2. Of those that a mesh axis runs over, the one named last changes fastest.
Arguments:
- source: bfloat16 [16384, 128], P('src'), may hold values from -6 to 6
- target: bfloat16 [32768, 128], P('tgt'), may hold values from -5 to 5
- start_map: float32 [128, 128], replicated, may hold values from -1 to 1
- warm_potential: float32 [32768], P('tgt'), may hold values from -60 to 24
Outputs:
- row_potential: float32 [16384], P('src')
- col_potential: float32 [32768], P('tgt')
- new_map: float32 [128, 128], replicated
All inputs are finite; a program needn't handle non-finite values.
Results may differ from a plain program's by a relative error of at most 0.0078.
Values sent between devices are 32-bit elements; how exact they have to be, the bound alone decides.
A program may use at most 64 MiB of HBM per device.

v0:
```python
import math

import jax
import jax.numpy as jnp
from jax import lax
from jax.sharding import PartitionSpec as P

ROUNDS = 3
NEWTON = 10


EPS = 0.05


def row_partials(rotated, target, col_pot, score_scale):
    row_count = rotated.shape[0]
    block_rows = math.gcd(row_count, 512)
    blocks = rotated.reshape(row_count // block_rows, block_rows, rotated.shape[1])

    def row_one_block(row_block):
        scores = (
            jnp.einsum("rd,cd->rc", row_block, target, preferred_element_type=jnp.float32)
            * score_scale
            + col_pot[None, :]
        )
        peak_val = jnp.max(scores, axis=1)
        totals = jnp.sum(jnp.exp(scores - peak_val[:, None]), axis=1)
        return (peak_val, totals)

    peak_val, totals = lax.map(row_one_block, blocks)
    return (peak_val.reshape(row_count), totals.reshape(row_count))


def col_partials(rotated, target, row_pot, score_scale):
    row_count = rotated.shape[0]
    block_rows = math.gcd(row_count, 512)
    blocks = rotated.reshape(row_count // block_rows, block_rows, rotated.shape[1])
    pots = row_pot.reshape(row_count // block_rows, block_rows)

    def col_one_block(inputs):
        row_block, pot_block = inputs
        scores = (
            jnp.einsum("rd,cd->rc", row_block, target, preferred_element_type=jnp.float32)
            * score_scale
            + pot_block[:, None]
        )
        peak_val = jnp.max(scores, axis=0)
        totals = jnp.sum(jnp.exp(scores - peak_val[None, :]), axis=0)
        return (peak_val, totals)

    peaks, totals = lax.map(col_one_block, (blocks, pots))
    peak_val = jnp.max(peaks, axis=0)
    return (peak_val, jnp.sum(totals * jnp.exp(peaks - peak_val[None, :]), axis=0))


def across_targets(peak_val, totals):
    global_peak = lax.pmax(peak_val, "tgt")
    totals = lax.psum(totals * jnp.exp(peak_val - global_peak), "tgt")
    peak_val = global_peak
    return peak_val + jnp.log(totals)


def across_sources(peak_val, totals):
    global_peak = lax.pmax(peak_val, "src")
    totals = lax.psum(totals * jnp.exp(peak_val - global_peak), "src")
    peak_val = global_peak
    return peak_val + jnp.log(totals)


def polar(matrix):
    iterate = matrix / jnp.sqrt(jnp.sum(matrix * matrix) + 1e-06)
    for newton_index in range(NEWTON):
        gram_matrix = jnp.dot(iterate.T, iterate, precision=lax.Precision.HIGHEST)
        iterate = 1.5 * iterate - 0.5 * jnp.dot(
            iterate, gram_matrix, precision=lax.Precision.HIGHEST
        )
    return iterate


def shards(source, target, start_map, warm_potential):
    width = source.shape[1]
    score_scale = 1.0 / (math.sqrt(width) * EPS)
    rows_all = source.shape[0] * lax.axis_size("src")
    cols_all = target.shape[0] * lax.axis_size("tgt")
    rotated = jnp.dot(
        source, start_map.astype(jnp.bfloat16), preferred_element_type=jnp.float32
    ).astype(jnp.bfloat16)
    col_pot = warm_potential
    for round_index in range(ROUNDS):
        row_pot = -math.log(rows_all) - across_targets(
            *row_partials(rotated, target, col_pot, score_scale)
        )
        col_pot = -math.log(cols_all) - across_sources(
            *col_partials(rotated, target, row_pot, score_scale)
        )
    row_lse = across_targets(*row_partials(rotated, target, col_pot, score_scale))
    row_pot = -math.log(rows_all) - row_lse
    rows_here = source.shape[0] // lax.axis_size("tgt")
    block_rows = math.gcd(rows_here * lax.axis_size("tgt"), 512)
    nblocks = rows_here * lax.axis_size("tgt") // block_rows

    def numerator_one_block(inputs):
        row_block, lse_block = inputs
        scores = (
            jnp.einsum("rd,cd->rc", row_block, target, preferred_element_type=jnp.float32)
            * score_scale
            + col_pot[None, :]
            - lse_block[:, None]
        )
        weights = jnp.exp(scores).astype(jnp.bfloat16)
        return jnp.dot(weights, target, preferred_element_type=jnp.float32)

    parts_out = lax.map(
        numerator_one_block,
        (rotated.reshape(nblocks, block_rows, width), row_lse.reshape(nblocks, block_rows)),
    )
    my_targets = lax.psum_scatter(
        parts_out.reshape(rows_here * lax.axis_size("tgt"), width),
        "tgt",
        scatter_dimension=0,
        tiled=True,
    )
    source_rows = lax.dynamic_slice_in_dim(source, lax.axis_index("tgt") * rows_here, rows_here, 0)
    partial_value = jnp.einsum(
        "rd,re->de", source_rows.astype(jnp.float32), my_targets, precision=lax.Precision.HIGHEST
    )
    covariance_sum = lax.psum(partial_value, ("src", "tgt"))
    new_map = polar(covariance_sum)
    return (EPS * row_pot, EPS * col_pot, new_map)


def solution(mesh):
    placed = (P("src", None), P("tgt", None), P(), P("tgt"))
    return jax.shard_map(
        shards, mesh=mesh, in_specs=placed, out_specs=(P("src"), P("tgt"), P()), check_vma=False
    )
```

profile of v0, /device:TPU:1, one launch (start us, length us, event | category | flops | bytes accessed | tf_op | source)
XLA Modules:
  0.0 1202.2 jit_solution(3626454813866031106)
XLA Ops:
  9.4 8.7 while.94
  9.4 1.5 fusion.139
  11.6 1.5 fusion.139
  13.7 1.5 fusion.139
  15.9 1.5 fusion.139
  18.1 65.3 %pmax.49 = f32[2048]{0:T(1024)S(1)} all-reduce(f32[2048]{0:T(1024)S(1)} %bitcast.221), channel_id=1, replica_groups=mesh['src'=8,'tgt'=32] {'tgt'}, use_global_device_ids=true, to_apply=%region_4.5 | all-reduce | flops 2048 | bytes 16384 | tf_op jit(solution)/shard_map/pmax | solution.py:57
  83.4 56.8 %psum.56 = f32[2048]{0:T(1024)S(1)} all-reduce(f32[2048]{0:T(1024)S(1)} %exponential_multiply_fusion.3), channel_id=1, replica_groups=mesh['src'=8,'tgt'=32] {'tgt'}, use_global_device_ids=true, to_apply=%region_5.6 | all-reduce | flops 2048 | bytes 16384 | tf_op jit(solution)/shard_map/psum | solution.py:58
  140.3 8.4 while.95
  146.6 1.4 fusion.141
  148.7 40.6 %pmax.50 = f32[1024]{0:T(1024)S(1)} all-reduce(f32[1024]{0:T(1024)S(1)} %reduce_max.90), channel_id=1, replica_groups=mesh['src'=8,'tgt'=32] {'src'}, use_global_device_ids=true, to_apply=%region_11.12 | all-reduce | flops 1024 | bytes 8192 | tf_op jit(solution)/shard_map/pmax | solution.py:64
  189.4 12.3 %psum.57 = f32[1024]{0:T(1024)S(1)} all-reduce(f32[1024]{0:T(1024)S(1)} %exponential_multiply_fusion.6), channel_id=1, replica_groups=mesh['src'=8,'tgt'=32] {'src'}, use_global_device_ids=true, to_apply=%region_13.14 | all-reduce | flops 1024 | bytes 8192 | tf_op jit(solution)/shard_map/psum | solution.py:65
  201.7 8.7 while.96
  201.7 1.5 fusion.143
  203.9 1.5 fusion.143
  206.1 1.5 fusion.143
  208.2 1.5 fusion.143
  210.4 58.5 %pmax.51 = f32[2048]{0:T(1024)S(1)} all-reduce(f32[2048]{0:T(1024)S(1)} %bitcast.223), channel_id=1, replica_groups=mesh['src'=8,'tgt'=32] {'tgt'}, use_global_device_ids=true, to_apply=%region_18.19 | all-reduce | flops 2048 | bytes 16384 | tf_op jit(solution)/shard_map/pmax | solution.py:57
  268.9 56.8 %psum.58 = f32[2048]{0:T(1024)S(1)} all-reduce(f32[2048]{0:T(1024)S(1)} %exponential_multiply_fusion.2), channel_id=1, replica_groups=mesh['src'=8,'tgt'=32] {'tgt'}, use_global_device_ids=true, to_apply=%region_19.20 | all-reduce | flops 2048 | bytes 16384 | tf_op jit(solution)/shard_map/psum | solution.py:58
  325.8 8.4 while.97
  332.1 1.4 fusion.145
  334.2 40.5 %pmax.52 = f32[1024]{0:T(1024)S(1)} all-reduce(f32[1024]{0:T(1024)S(1)} %reduce_max.91), channel_id=1, replica_groups=mesh['src'=8,'tgt'=32] {'src'}, use_global_device_ids=true, to_apply=%region_25.26 | all-reduce | flops 1024 | bytes 8192 | tf_op jit(solution)/shard_map/pmax | solution.py:64
  374.8 12.4 %psum.59 = f32[1024]{0:T(1024)S(1)} all-reduce(f32[1024]{0:T(1024)S(1)} %exponential_multiply_fusion.5), channel_id=1, replica_groups=mesh['src'=8,'tgt'=32] {'src'}, use_global_device_ids=true, to_apply=%region_27.28 | all-reduce | flops 1024 | bytes 8192 | tf_op jit(solution)/shard_map/psum | solution.py:65
  387.2 8.7 while.98
  387.2 1.5 fusion.147
  389.4 1.5 fusion.147
  391.6 1.5 fusion.147
  393.8 1.5 fusion.147
  395.9 59.2 %pmax.53 = f32[2048]{0:T(1024)S(1)} all-reduce(f32[2048]{0:T(1024)S(1)} %bitcast.225), channel_id=1, replica_groups=mesh['src'=8,'tgt'=32] {'tgt'}, use_global_device_ids=true, to_apply=%region_32.33 | all-reduce | flops 2048 | bytes 16384 | tf_op jit(solution)/shard_map/pmax | solution.py:57
  455.1 57.0 %psum.60 = f32[2048]{0:T(1024)S(1)} all-reduce(f32[2048]{0:T(1024)S(1)} %exponential_multiply_fusion.1), channel_id=1, replica_groups=mesh['src'=8,'tgt'=32] {'tgt'}, use_global_device_ids=true, to_apply=%region_33.34 | all-reduce | flops 2048 | bytes 16384 | tf_op jit(solution)/shard_map/psum | solution.py:58
  512.2 8.4 while.99
  520.6 39.6 %pmax.54 = f32[1024]{0:T(1024)S(1)} all-reduce(f32[1024]{0:T(1024)S(1)} %reduce_max.92), channel_id=1, replica_groups=mesh['src'=8,'tgt'=32] {'src'}, use_global_device_ids=true, to_apply=%region_39.40 | all-reduce | flops 1024 | bytes 8192 | tf_op jit(solution)/shard_map/pmax | solution.py:64
  560.3 12.4 %psum.61 = f32[1024]{0:T(1024)S(1)} all-reduce(f32[1024]{0:T(1024)S(1)} %exponential_multiply_fusion.4), channel_id=1, replica_groups=mesh['src'=8,'tgt'=32] {'src'}, use_global_device_ids=true, to_apply=%region_41.42 | all-reduce | flops 1024 | bytes 8192 | tf_op jit(solution)/shard_map/psum | solution.py:65
  573.3 8.7 while.100
  573.3 1.5 fusion.151
  575.5 1.5 fusion.151
  577.7 1.5 fusion.151
  579.9 1.5 fusion.151
  582.1 59.2 %pmax.55 = f32[2048]{0:T(1024)S(1)} all-reduce(f32[2048]{0:T(1024)S(1)} %bitcast.227), channel_id=1, replica_groups=mesh['src'=8,'tgt'=32] {'tgt'}, use_global_device_ids=true, to_apply=%region_46.47 | all-reduce | flops 2048 | bytes 16384 | tf_op jit(solution)/shard_map/pmax | solution.py:57
  641.3 57.0 %psum.62 = f32[2048]{0:T(1024)S(1)} all-reduce(f32[2048]{0:T(1024)S(1)} %exponential_multiply_fusion), channel_id=1, replica_groups=mesh['src'=8,'tgt'=32] {'tgt'}, use_global_device_ids=true, to_apply=%region_47.48 | all-reduce | flops 2048 | bytes 16384 | tf_op jit(solution)/shard_map/psum | solution.py:58
  698.9 10.4 while.101
  698.9 2.6 fusion.155
  701.5 2.6 fusion.155
  704.1 2.6 fusion.155
  706.7 2.6 fusion.155
  709.6 228.3 %reduce-scatter.2.cloned.1.call-done = f32[64,128]{1,0:T(8,128)} async-done(((f32[2048,128]{1,0:T(8,128)}), f32[64,128]{1,0:T(8,128)}) %reduce-scatter.2.cloned.1.call-update) | async-done | bytes 32784 | tf_op jit(solution)/shard_map/reduce_scatter | solution.py:117
  937.9 1.6 fusion.60
  939.5 246.2 %all-reduce.2.cloned.1.call-done = f32[128,128]{1,0:T(8,128)} async-done(((f32[128,128]{1,0:T(8,128)}), f32[128,128]{1,0:T(8,128)}) %all-reduce.2.cloned.1.call-update) | async-done | bytes 65552 | tf_op jit(solution)/shard_map/psum | solution.py:127
  1185.8 1.5 multiply_reduce_fusion
  (192 shorter events, 43.9 us)
Async XLA Ops:
  7.2 1.0 copy-start
  7.2 930.7 %reduce-scatter.2.cloned.1.call-start = ((), (), s32[]{:S(2)}) async-start(), calls=%async_computation.1 | async-start | bytes 1081344 | tf_op jit(solution)/shard_map/reduce_scatter | solution.py:117
  9.4 1.5 copy-start.1
  11.6 1.5 copy-start.1
  13.7 1.5 copy-start.1
  15.9 1.5 copy-start.1
  709.4 476.4 %all-reduce.2.cloned.1.call-start = ((), (), s32[]{:S(2)}) async-start(), calls=%async_computation.2 | async-start | bytes 131072 | tf_op jit(solution)/shard_map/psum | solution.py:127
Sparse Core Ops, SparseCore 0:
  709.5 228.3 reduce-scatter.1
  944.0 241.7 all-reduce.1
where the time goes:
time: 1200 us
  blocking collectives  628 us (52%)
  waiting for transfers between devices  475 us (40%)
  matrix products  60.8 us (5%)
  other arithmetic  18 us (2%)
  between operations  15.3 us (1%)
    psum x1, waiting for transfers between devices, shards(): covariance_sum = lax.psum(partial_value, ('src', 'tgt'))  246 us
    pmax x4, blocking collectives, across_targets(): global_peak = lax.pmax(peak_val, 'tgt')  242 us
    reduce_scatter x1, waiting for transfers between devices, shards(): lax.psum_scatter(parts_out.reshape(rows_here * lax.axis_size('tgt'), widt...  228 us
    psum x4, blocking collectives, across_targets(): totals = lax.psum(totals * jnp.exp(peak_val - global_peak), 'tgt')  228 us
    pmax x3, blocking collectives, across_sources(): global_peak = lax.pmax(peak_val, 'src')  121 us
    psum x3, blocking collectives, across_sources(): totals = lax.psum(totals * jnp.exp(peak_val - global_peak), 'src')  37.1 us
  transfers between devices with their start and end apart: 2, of which 2 were waited for; matrix products, arithmetic and copies ran while one was open for 0% of the time, Pallas kernels for 0%

commit v1 on v0

v1 whole, which is shorter than its diff:
```python
import functools
import math

import jax
import jax.numpy as jnp
from jax import lax
from jax.experimental import pallas as pl
from jax.experimental.pallas import tpu as pltpu
from jax.sharding import PartitionSpec as P

ROUNDS = 3
NEWTON = 10
EPS = 0.05
LN2 = math.log(2.0)
MESH = pl.DeviceIdType.MESH
F32 = jnp.float32
BF16 = jnp.bfloat16
NX, NY, NZ, NC = 4, 4, 8, 2
NSRC = NY * NC
L = 128


def split(value):
    high = value.astype(BF16)
    low = (value - high.astype(F32)).astype(BF16)
    return high, low


def dot_nt(a, b):
    return lax.dot_general(a, b, (((1,), (1,)), ((), ())), preferred_element_type=F32)


def dot_nn(a, b):
    return jnp.dot(a, b, preferred_element_type=F32)


def lse2(parts):
    peak = parts[0]
    for part in parts[1:]:
        peak = jnp.maximum(peak, part)
    total = jnp.exp2(parts[0] - peak)
    for part in parts[1:]:
        total = total + jnp.exp2(part - peak)
    return peak + jnp.log2(total)


def total_of(parts):
    total = parts[0]
    for part in parts[1:]:
        total = total + part
    return total


def kernel(
    rows_all,
    cols_all,
    source_ref,
    target_ref,
    map_ref,
    warm_ref,
    row_out,
    col_out,
    map_out,
    rot,
    e_f32,
    e_b16,
    src_t,
    tgt_t,
    bary,
    u_t,
    cross,
    row_z,
    row_x,
    col_s,
    cross_s,
    cross_z,
    cross_x,
    cross_g,
    send_sem,
    recv_sem,
):
    rows, width = source_ref.shape
    cols = target_ref.shape[0]
    nb, nk = rows // L, cols // L
    scale2 = 1.0 / (math.sqrt(width) * EPS) / LN2
    me_s = lax.axis_index("src")
    me_t = lax.axis_index("tgt")
    me_x, me_z = me_t // NZ, lax.rem(me_t, NZ)
    peers_s = [(lax.rem(me_s + k, NSRC), me_t) for k in (4, 3, 5, 2, 6, 1, 7)]
    peers_z = [(me_s, me_x * NZ + lax.rem(me_z + k, NZ)) for k in (4, 3, 5, 2, 6, 1, 7)]
    peers_x = [(me_s, lax.rem(me_x + k, NX) * NZ + me_z) for k in (2, 1, 3)]

    barrier = pltpu.get_barrier_semaphore()
    everyone = peers_s + peers_z + peers_x
    for peer in everyone:
        pl.semaphore_signal(barrier, inc=1, device_id=peer, device_id_type=MESH)

    pending = []

    def send(phase, buf, me, peers):
        for peer in peers:
            pltpu.make_async_remote_copy(
                src_ref=buf.at[me],
                dst_ref=buf.at[me],
                send_sem=send_sem.at[phase],
                recv_sem=recv_sem.at[phase],
                device_id=peer,
                device_id_type=MESH,
            ).start()
        others = buf.at[pl.ds(0, len(peers))]
        done = pltpu.make_async_remote_copy(
            src_ref=others,
            dst_ref=others,
            send_sem=send_sem.at[phase],
            recv_sem=recv_sem.at[phase],
            device_id=peers[0],
            device_id_type=MESH,
        )
        pending.append(done)
        return done

    lane = lax.broadcasted_iota(jnp.int32, (L, L), 1)
    zero_tile = jnp.zeros((L, L), F32)

    def chunk(k):
        return pl.ds(k * L, L)

    rot[...] = dot_nn(source_ref[...], map_ref[...].astype(BF16)).astype(BF16)
    warm2 = warm_ref[...] * (1.0 / LN2)
    wide = 256
    for k in range(cols // wide):
        part = target_ref[pl.ds(k * wide, wide), :]
        warm_part = warm2[:, k * wide : (k + 1) * wide]

        def score_block(a, carry):
            block = rot[pl.ds(pl.multiple_of(a * 512, 512), 512), :]
            e_f32[pl.ds(a * 4, 4), :, pl.ds(k * wide, wide)] = (
                dot_nt(block, part) * scale2 + warm_part
            ).reshape(4, L, wide)
            return carry

        lax.fori_loop(0, rows // 512, score_block, 0)

    def first_row(a, acc):
        peak = e_f32[a, :, chunk(0)]
        for k in range(1, nk):
            peak = jnp.maximum(peak, e_f32[a, :, chunk(k)])
        peak = jnp.max(peak, axis=1, keepdims=True)
        total = jnp.exp2(e_f32[a, :, chunk(0)] - peak)
        for k in range(1, nk):
            total = total + jnp.exp2(e_f32[a, :, chunk(k)] - peak)
        total = jnp.sum(total, axis=1, keepdims=True)
        return jnp.where(lane == a, peak + jnp.log2(total), acc)

    first = lax.fori_loop(0, nb, first_row, zero_tile, unroll=2)
    pl.semaphore_wait(barrier, len(everyone))

    def row_reduce(index, tile, combine, meanwhile=None, meanwhile2=None):
        row_z[index, me_z] = tile.T[:nb]
        done = send(3 * index, row_z.at[index], me_z, peers_z)
        if meanwhile is not None:
            meanwhile()
        done.wait_recv()
        row_x[index, me_x] = combine([row_z[index, i] for i in range(NZ)])
        done = send(3 * index + 1, row_x.at[index], me_x, peers_x)
        if meanwhile2 is not None:
            meanwhile2()
        done.wait_recv()
        return combine([row_x[index, i] for i in range(NX)])

    def col_reduce(index, combine):
        done = send(3 * index + 2, col_s.at[index], me_s, peers_s)
        done.wait_recv()
        return combine([col_s[index, i] for i in range(NSRC)])

    def spread(value):
        u_t[...] = jnp.concatenate([value, jnp.zeros((L - nb, L), F32)], axis=0).T

    def column_of(a):
        return jnp.sum(jnp.where(lane == a, u_t[...], 0.0), axis=1, keepdims=True)

    def fold(tile, op):
        parts = [tile[8 * i : 8 * i + 8] for i in range(L // 8)]
        while len(parts) > 1:
            parts = [op(parts[i], parts[i + 1]) for i in range(0, len(parts), 2)]
        return parts[0]

    def transposes():
        def one_source(a, carry):
            block = source_ref[pl.ds(pl.multiple_of(a * L, L), L), :].astype(F32)
            src_t[a] = block.T
            return carry

        lax.fori_loop(0, nb, one_source, 0)

        def one_target(a, carry):
            block = target_ref[pl.ds(pl.multiple_of(a * L, L), L), :].astype(F32)
            tgt_t[a] = block.T
            return carry

        lax.fori_loop(0, nk, one_target, 0)

    row_lse = row_reduce(0, first, lse2, transposes)
    f_first = -math.log2(rows_all) - row_lse
    spread(f_first)

    def first_col_peak(a, accs):
        f_col = column_of(a)
        return tuple(
            jnp.maximum(accs[k], fold(e_f32[a, :, chunk(k)] + f_col, jnp.maximum))
            for k in range(nk)
        )

    peaks = lax.fori_loop(
        0, nb, first_col_peak, tuple(jnp.full((8, L), -jnp.inf, F32) for _ in range(nk))
    )
    peaks = [jnp.max(p, axis=0, keepdims=True) for p in peaks]

    def first_col_sum(a, accs):
        f_col = column_of(a)
        out = []
        for k in range(nk):
            e_val = jnp.exp2((e_f32[a, :, chunk(k)] + f_col) - peaks[k])
            e_f32[a, :, chunk(k)] = e_val
            e_b16[a, :, chunk(k)] = e_val.astype(BF16)
            out.append(accs[k] + fold(e_val, jnp.add))
        return tuple(out)

    zeros = tuple(jnp.zeros((8, L), F32) for _ in range(nk))
    sums = lax.fori_loop(0, nb, first_col_sum, zeros)
    for k in range(nk):
        total = jnp.sum(sums[k], axis=0, keepdims=True)
        col_s[0, me_s, :, chunk(k)] = peaks[k] + jnp.log2(total)
    col_lse = col_reduce(0, lse2)
    g_first = warm2 - math.log2(cols_all) - col_lse
    local_weight = jnp.concatenate(
        [
            jnp.exp2(peaks[k] - col_lse[:, k * L : (k + 1) * L] - math.log2(cols_all))
            for k in range(nk)
        ],
        axis=1,
    )

    def row_pass(weight):
        weights = [weight[:, k * L : (k + 1) * L] for k in range(nk)]

        def body(a, acc):
            total = e_f32[a, :, chunk(0)] * weights[0]
            for k in range(1, nk):
                total = total + e_f32[a, :, chunk(k)] * weights[k]
            total = jnp.sum(total, axis=1, keepdims=True)
            return jnp.where(lane == a, total, acc)

        return lax.fori_loop(0, nb, body, zero_tile, unroll=2)

    def col_pass(index):
        def body(a, accs):
            u_col = column_of(a)
            return tuple(
                accs[k] + fold(e_f32[a, :, chunk(k)] * u_col, jnp.add) for k in range(nk)
            )

        sums = lax.fori_loop(0, nb, body, zeros, unroll=2)
        for k in range(nk):
            total = jnp.sum(sums[k], axis=0, keepdims=True)
            col_s[index, me_s, :, chunk(k)] = total * local_weight[:, k * L : (k + 1) * L]

    weight = local_weight
    v_val = None
    for index in range(1, ROUNDS):
        mass = row_reduce(index, row_pass(weight), total_of)
        spread(1.0 / (mass * rows_all))
        col_pass(index)
        v_val = 1.0 / (col_reduce(index, total_of) * cols_all)
        weight = local_weight * v_val

    def barycentric():
        col_out[...] = (EPS * LN2) * (g_first + jnp.log2(v_val))
        pieces = [split(tgt_t[k] * weight[:, k * L : (k + 1) * L]) for k in range(nk)]
        both = jnp.concatenate(
            [
                jnp.concatenate([p[0] for p in pieces], axis=1),
                jnp.concatenate([p[1] for p in pieces], axis=1),
            ],
            axis=0,
        )

        def body(a, carry):
            block = e_b16[pl.ds(a * 4, 4)].reshape(4 * L, cols)
            out = dot_nt(block, both)
            high, low = split(out[:, :width] + out[:, width:])
            start = pl.multiple_of(a * 4 * L, 4 * L)
            bary[pl.ds(start, 4 * L), pl.ds(0, width)] = high
            bary[pl.ds(start, 4 * L), pl.ds(width, width)] = low
            return carry

        lax.fori_loop(0, nb // 4, body, 0)

    mass = row_reduce(ROUNDS, row_pass(weight), total_of, barycentric)
    row_out[...] = (EPS * LN2) * (f_first - math.log2(rows_all) - jnp.log2(mass))
    inverse = 1.0 / mass

    pieces = [split(src_t[a] * inverse[a : a + 1, :]) for a in range(nb)]
    stacked = jnp.concatenate(
        [
            jnp.concatenate([p[0] for p in pieces], axis=1),
            jnp.concatenate([p[1] for p in pieces], axis=1),
        ],
        axis=0,
    )
    out = dot_nn(stacked, bary[...])
    cross[...] = (
        out[:width, :width] + out[:width, width:] + out[width:, :width] + out[width:, width:]
    ).reshape(NSRC, width // NSRC, width)

    phase = 3 * ROUNDS + 2
    cross_s[me_s] = cross[me_s]
    for peer in peers_s:
        pltpu.make_async_remote_copy(
            src_ref=cross.at[peer[0]],
            dst_ref=cross_s.at[me_s],
            send_sem=send_sem.at[phase],
            recv_sem=recv_sem.at[phase],
            device_id=peer,
            device_id_type=MESH,
        ).start()
    others = cross_s.at[pl.ds(0, len(peers_s))]
    done = pltpu.make_async_remote_copy(
        src_ref=others,
        dst_ref=others,
        send_sem=send_sem.at[phase],
        recv_sem=recv_sem.at[phase],
        device_id=peers_s[0],
        device_id_type=MESH,
    )
    pending.append(done)
    done.wait_recv()
    cross_z[me_z] = total_of([cross_s[i] for i in range(NSRC)])
    send(phase + 1, cross_z, me_z, peers_z).wait_recv()
    cross_x[me_x] = total_of([cross_z[i] for i in range(NZ)])
    send(phase + 2, cross_x, me_x, peers_x).wait_recv()
    cross_g[me_s] = total_of([cross_x[i] for i in range(NX)])
    send(phase + 3, cross_g, me_s, peers_s).wait_recv()

    matrix = cross_g[...].reshape(width, width)
    norm = jnp.sum(jnp.sum(matrix * matrix, axis=1, keepdims=True), axis=0, keepdims=True)
    iterate = matrix / jnp.sqrt(norm + 1e-06)

    def newton(_, iterate):
        high, low = split(iterate)
        pair = jnp.concatenate([high, low], axis=1)
        twice = jnp.concatenate(
            [jnp.concatenate([high, high], axis=1), jnp.concatenate([low, low], axis=1)], axis=0
        )
        gram = dot_nt(pair, twice)
        gram = gram[:, :width] + gram[:, width:]
        pair_g = jnp.concatenate(split(gram), axis=1)
        stack = jnp.concatenate([pair, pair], axis=0)
        prod = dot_nn(pair_g, stack)
        return 1.5 * iterate - 0.5 * (prod[:, :width] + prod[:, width:])

    map_out[...] = lax.fori_loop(0, NEWTON, newton, iterate)
    for done in pending:
        done.wait_send()


def shards(source, target, start_map, warm_potential):
    rows, width = source.shape
    cols = target.shape[0]
    rows_all, cols_all = rows * lax.axis_size("src"), cols * lax.axis_size("tgt")
    nb, nk = rows // L, cols // L
    phases = 3 * ROUNDS + 2 + 4
    vmem = pltpu.VMEM
    row_pot, col_pot, new_map = pl.pallas_call(
        functools.partial(kernel, rows_all, cols_all),
        out_shape=(
            jax.ShapeDtypeStruct((nb, L), F32),
            jax.ShapeDtypeStruct((1, cols), F32),
            jax.ShapeDtypeStruct((width, width), F32),
        ),
        in_specs=[pl.BlockSpec(memory_space=vmem)] * 4,
        out_specs=[pl.BlockSpec(memory_space=vmem)] * 3,
        scratch_shapes=[
            vmem((rows, width), BF16),
            vmem((nb, L, cols), F32),
            vmem((nb, L, cols), BF16),
            vmem((nb, width, L), F32),
            vmem((nk, width, L), F32),
            vmem((rows, 2 * width), BF16),
            vmem((L, L), F32),
            vmem((NSRC, width // NSRC, width), F32),
            vmem((ROUNDS + 1, NZ, nb, L), F32),
            vmem((ROUNDS + 1, NX, nb, L), F32),
            vmem((ROUNDS, NSRC, 1, cols), F32),
            vmem((NSRC, width // NSRC, width), F32),
            vmem((NZ, width // NSRC, width), F32),
            vmem((NX, width // NSRC, width), F32),
            vmem((NSRC, width // NSRC, width), F32),
            pltpu.SemaphoreType.DMA((phases,)),
            pltpu.SemaphoreType.DMA((phases,)),
        ],
        compiler_params=pltpu.CompilerParams(
            collective_id=0, has_side_effects=True, vmem_limit_bytes=48 << 20
        ),
        name="sinkhorn_refit",
    )(source, target, start_map, warm_potential.reshape(1, cols))
    return row_pot.reshape(rows), col_pot.reshape(cols), new_map


def solution(mesh):
    placed = (P("src", None), P("tgt", None), P(), P("tgt"))
    return jax.shard_map(
        shards,
        mesh=mesh,
        in_specs=placed,
        out_specs=(P("src"), P("tgt"), P()),
        check_vma=False,
    )
```

time: 1200 us -> 93.7 us (0.08)
  blocking collectives: 628 us -> 0 us
  waiting for transfers between devices: 475 us -> 0 us
  Pallas kernels: 0 us -> 87.5 us
  matrix products: 60.8 us -> 0 us
  other arithmetic: 18 us -> 0 us
  between operations: 15.3 us -> 0.65 us
    pmax x7 -> x0, blocking collectives: 363 us -> none  [the longest x4 242 us: across_targets(): global_peak = lax.pmax(peak_val, 'tgt')]
    psum x7 -> x0, blocking collectives: 265 us -> none  [the longest x4 228 us: across_targets(): totals = lax.psum(totals * jnp.exp(peak_val - global_peak), 'tgt')]
    psum x1 -> x0, waiting for transfers between devices: 246 us -> none  [shards(): covariance_sum = lax.psum(partial_value, ('src', 'tgt'))]
    reduce_scatter x1 -> x0, waiting for transfers between devices: 228 us -> none  [shards(): lax.psum_scatter(parts_out.reshape(rows_here * lax.axis_size('tgt'), widt...]
    pallas_call x0 -> x1, Pallas kernels: none -> 87.5 us  [shards(): pl.pallas_call(functools.partial(kernel, rows_all, cols_all), out_shape=(...]
    dot_general x54 -> x0, matrix products: 60.8 us -> none  [the longest x16 23.5 us: row_one_block(): jnp.einsum('rd,cd->rc', row_block, target, preferred_element_type=jnp.flo...]
    reduce_sum x32 -> x0, other arithmetic: 16.7 us -> none  [the longest x16 9.37 us: row_one_block(): totals = jnp.sum(jnp.exp(scores - peak_val[:, None]), axis=1)]
  transfers between devices with their start and end apart: 2 -> 0, of which waited for: 2 -> 0; matrix products, arithmetic and copies ran while one was open for 0% -> 0% of each run, Pallas kernels for 0% -> 0%
where the time goes in v1:
time: 93.7 us; the launch traced here: 93.5 us
  Pallas kernels  87.5 us (93%)
  local copies, waits for them, and re-layouts  5.33 us (6%)
    pallas_call x1, Pallas kernels, shards(): pl.pallas_call(functools.partial(kernel, rows_all, cols_all), out_shape=(...  87.5 us
    unnamed x11, local copies, waits for them, and re-layouts  5.33 us

profile of v1, /device:TPU:1, one launch (start us, length us, event | category | flops | bytes accessed | tf_op | source)
XLA Modules:
  0.0 93.5 jit_solution(1956081253081396285)
XLA Ops:
  0.6 0.0 copy-start
  0.6 1.0 %copy-done = bf16[2048,128]{1,0:T(8,128)(2,1)S(1)} copy-done((bf16[2048,128]{1,0:T(8,128)(2,1)S(1)}, bf16[2048,128]{1,0:T(8,128)(2,1)}, u32[]{:S(2)}) %copy-start) | copy-done | bytes 524312
  1.7 0.0 copy-start.1
  1.7 0.9 %copy-done.1 = bf16[1024,128]{1,0:T(8,128)(2,1)S(1)} copy-done((bf16[1024,128]{1,0:T(8,128)(2,1)S(1)}, bf16[1024,128]{1,0:T(8,128)(2,1)}, u32[]{:S(2)}) %copy-start.1) | copy-done | bytes 262168
  2.6 0.0 copy-start.2
  2.6 0.8 copy-done.2
  3.5 0.0 copy-start.3
  3.5 0.7 copy-done.3
  4.2 87.5 %sinkhorn_refit.1 = (f32[16,128]{1,0:T(8,128)S(1)}, f32[1,1024]{1,0:T(1,128)S(1)}, f32[128,128]{1,0:T(8,128)S(1)}) custom-call(bf16[2048,128]{1,0:T(8,128)(2,1)S(1)} %copy-done, bf16[1024,128]{1,0:T(8,128)(2,1)S(1)} %copy-done.1, f32[128,128]{1,0:T(8,128)S(1)} %copy-done.2, f32[1,1024]{1,0:T(1,128)S(1)} %bitcast.4), custom_call_target="tpu_custom_call" | custom-call | tf_op jit(solution)/shard_map/sinkhorn_refit/pallas_call | solution.py:374
  91.7 0.6 copy.10
  92.3 0.6 copy.11
  92.9 0.6 copy.12
Async XLA Ops:
  0.6 1.0 %copy-start = (bf16[2048,128]{1,0:T(8,128)(2,1)S(1)}, bf16[2048,128]{1,0:T(8,128)(2,1)}, u32[]{:S(2)}) copy-start(bf16[2048,128]{1,0:T(8,128)(2,1)} %source_ref.1) | copy-start | bytes 1572868
  1.7 0.9 %copy-start.1 = (bf16[1024,128]{1,0:T(8,128)(2,1)S(1)}, bf16[1024,128]{1,0:T(8,128)(2,1)}, u32[]{:S(2)}) copy-start(bf16[1024,128]{1,0:T(8,128)(2,1)} %target_ref.1) | copy-start | bytes 786436
  2.6 0.8 copy-start.2
  3.5 0.7 copy-start.3

commit v2 on v1

--- a/solution.py
+++ b/solution.py
@@ -54,13 +54,17 @@
 def kernel(
     rows_all,
     cols_all,
+    source_hbm,
+    target_hbm,
+    map_hbm,
+    warm_hbm,
+    row_out,
+    col_out,
+    cross_g,
     source_ref,
     target_ref,
     map_ref,
     warm_ref,
-    row_out,
-    col_out,
-    map_out,
     rot,
     e_f32,
     e_b16,
@@ -75,10 +79,23 @@
     cross_s,
     cross_z,
     cross_x,
-    cross_g,
     send_sem,
     recv_sem,
+    load_sem,
 ):
+    loads = [
+        pltpu.make_async_copy(hbm, ref, load_sem.at[i])
+        for i, (hbm, ref) in enumerate(
+            [
+                (map_hbm, map_ref),
+                (source_hbm, source_ref),
+                (target_hbm, target_ref),
+                (warm_hbm, warm_ref),
+            ]
+        )
+    ]
+    for load in loads:
+        load.start()
     rows, width = source_ref.shape
     cols = target_ref.shape[0]
     nb, nk = rows // L, cols // L
@@ -125,7 +142,11 @@
     def chunk(k):
         return pl.ds(k * L, L)
 
+    loads[0].wait()
+    loads[1].wait()
     rot[...] = dot_nn(source_ref[...], map_ref[...].astype(BF16)).astype(BF16)
+    loads[2].wait()
+    loads[3].wait()
     warm2 = warm_ref[...] * (1.0 / LN2)
     wide = 256
     for k in range(cols // wide):
@@ -139,7 +160,7 @@
             ).reshape(4, L, wide)
             return carry
 
-        lax.fori_loop(0, rows // 512, score_block, 0)
+        lax.fori_loop(0, rows // 512, score_block, 0, unroll=4)
 
     def first_row(a, acc):
         peak = e_f32[a, :, chunk(0)]
@@ -152,7 +173,7 @@
         total = jnp.sum(total, axis=1, keepdims=True)
         return jnp.where(lane == a, peak + jnp.log2(total), acc)
 
-    first = lax.fori_loop(0, nb, first_row, zero_tile, unroll=2)
+    first = lax.fori_loop(0, nb, first_row, zero_tile, unroll=4)
     pl.semaphore_wait(barrier, len(everyone))
 
     def row_reduce(index, tile, combine, meanwhile=None, meanwhile2=None):
@@ -212,7 +233,7 @@
         )
 
     peaks = lax.fori_loop(
-        0, nb, first_col_peak, tuple(jnp.full((8, L), -jnp.inf, F32) for _ in range(nk))
+        0, nb, first_col_peak, tuple(jnp.full((8, L), -jnp.inf, F32) for _ in range(nk)), unroll=8
     )
     peaks = [jnp.max(p, axis=0, keepdims=True) for p in peaks]
 
@@ -227,7 +248,7 @@
         return tuple(out)
 
     zeros = tuple(jnp.zeros((8, L), F32) for _ in range(nk))
-    sums = lax.fori_loop(0, nb, first_col_sum, zeros)
+    sums = lax.fori_loop(0, nb, first_col_sum, zeros, unroll=4)
     for k in range(nk):
         total = jnp.sum(sums[k], axis=0, keepdims=True)
         col_s[0, me_s, :, chunk(k)] = peaks[k] + jnp.log2(total)
@@ -251,7 +272,7 @@
             total = jnp.sum(total, axis=1, keepdims=True)
             return jnp.where(lane == a, total, acc)
 
-        return lax.fori_loop(0, nb, body, zero_tile, unroll=2)
+        return lax.fori_loop(0, nb, body, zero_tile, unroll=16)
 
     def col_pass(index):
         def body(a, accs):
@@ -260,7 +281,7 @@
                 accs[k] + fold(e_f32[a, :, chunk(k)] * u_col, jnp.add) for k in range(nk)
             )
 
-        sums = lax.fori_loop(0, nb, body, zeros, unroll=2)
+        sums = lax.fori_loop(0, nb, body, zeros, unroll=16)
         for k in range(nk):
             total = jnp.sum(sums[k], axis=0, keepdims=True)
             col_s[index, me_s, :, chunk(k)] = total * local_weight[:, k * L : (k + 1) * L]
@@ -294,7 +315,7 @@
             bary[pl.ds(start, 4 * L), pl.ds(width, width)] = low
             return carry
 
-        lax.fori_loop(0, nb // 4, body, 0)
+        lax.fori_loop(0, nb // 4, body, 0, unroll=2)
 
     mass = row_reduce(ROUNDS, row_pass(weight), total_of, barycentric)
     row_out[...] = (EPS * LN2) * (f_first - math.log2(rows_all) - jnp.log2(mass))
@@ -342,7 +363,20 @@
     cross_g[me_s] = total_of([cross_x[i] for i in range(NX)])
     send(phase + 3, cross_g, me_s, peers_s).wait_recv()
 
-    matrix = cross_g[...].reshape(width, width)
+    for done in pending:
+        done.wait_send()
+
+
+def polar_kernel(cross_ref, row_ref, col_ref, row_out, col_out, map_out, result, sems):
+    stores = [
+        pltpu.make_async_copy(row_ref, row_out, sems.at[0]),
+        pltpu.make_async_copy(col_ref, col_out, sems.at[1]),
+        pltpu.make_async_copy(result, map_out, sems.at[2]),
+    ]
+    stores[0].start()
+    stores[1].start()
+    width = result.shape[0]
+    matrix = cross_ref[...].reshape(width, width)
     norm = jnp.sum(jnp.sum(matrix * matrix, axis=1, keepdims=True), axis=0, keepdims=True)
     iterate = matrix / jnp.sqrt(norm + 1e-06)
 
@@ -359,9 +393,10 @@
         prod = dot_nn(pair_g, stack)
         return 1.5 * iterate - 0.5 * (prod[:, :width] + prod[:, width:])
 
-    map_out[...] = lax.fori_loop(0, NEWTON, newton, iterate)
-    for done in pending:
-        done.wait_send()
+    result[...] = lax.fori_loop(0, NEWTON, newton, iterate)
+    stores[2].start()
+    for store in stores:
+        store.wait()
 
 
 def shards(source, target, start_map, warm_potential):
@@ -371,16 +406,18 @@
     nb, nk = rows // L, cols // L
     phases = 3 * ROUNDS + 2 + 4
     vmem = pltpu.VMEM
-    row_pot, col_pot, new_map = pl.pallas_call(
+    pots = (jax.ShapeDtypeStruct((nb, L), F32), jax.ShapeDtypeStruct((1, cols), F32))
+    part_shape = (NSRC, width // NSRC, width)
+    row_pot, col_pot, cross = pl.pallas_call(
         functools.partial(kernel, rows_all, cols_all),
-        out_shape=(
-            jax.ShapeDtypeStruct((nb, L), F32),
-            jax.ShapeDtypeStruct((1, cols), F32),
-            jax.ShapeDtypeStruct((width, width), F32),
-        ),
-        in_specs=[pl.BlockSpec(memory_space=vmem)] * 4,
+        out_shape=(*pots, jax.ShapeDtypeStruct(part_shape, F32)),
+        in_specs=[pl.BlockSpec(memory_space=pl.ANY)] * 4,
         out_specs=[pl.BlockSpec(memory_space=vmem)] * 3,
         scratch_shapes=[
+            vmem((rows, width), BF16),
+            vmem((cols, width), BF16),
+            vmem((width, width), F32),
+            vmem((1, cols), F32),
             vmem((rows, width), BF16),
             vmem((nb, L, cols), F32),
             vmem((nb, L, cols), BF16),
@@ -388,22 +425,30 @@
             vmem((nk, width, L), F32),
             vmem((rows, 2 * width), BF16),
             vmem((L, L), F32),
-            vmem((NSRC, width // NSRC, width), F32),
+            vmem(part_shape, F32),
             vmem((ROUNDS + 1, NZ, nb, L), F32),
             vmem((ROUNDS + 1, NX, nb, L), F32),
             vmem((ROUNDS, NSRC, 1, cols), F32),
-            vmem((NSRC, width // NSRC, width), F32),
-            vmem((NZ, width // NSRC, width), F32),
-            vmem((NX, width // NSRC, width), F32),
-            vmem((NSRC, width // NSRC, width), F32),
+            vmem(part_shape, F32),
+            vmem((NZ, *part_shape[1:]), F32),
+            vmem((NX, *part_shape[1:]), F32),
             pltpu.SemaphoreType.DMA((phases,)),
             pltpu.SemaphoreType.DMA((phases,)),
+            pltpu.SemaphoreType.DMA((4,)),
         ],
         compiler_params=pltpu.CompilerParams(
-            collective_id=0, has_side_effects=True, vmem_limit_bytes=48 << 20
+            collective_id=0, has_side_effects=True, vmem_limit_bytes=60 << 20
         ),
-        name="sinkhorn_refit",
+        name="sinkhorn",
     )(source, target, start_map, warm_potential.reshape(1, cols))
+    row_pot, col_pot, new_map = pl.pallas_call(
+        polar_kernel,
+        out_shape=(*pots, jax.ShapeDtypeStruct((width, width), F32)),
+        in_specs=[pl.BlockSpec(memory_space=vmem)] * 3,
+        out_specs=[pl.BlockSpec(memory_space=pl.ANY)] * 3,
+        scratch_shapes=[vmem((width, width), F32), pltpu.SemaphoreType.DMA((3,))],
+        name="polar",
+    )(cross, row_pot, col_pot)
     return row_pot.reshape(rows), col_pot.reshape(cols), new_map
 
 

time: 93.7 us -> 83.9 us (0.90)
  local copies, waits for them, and re-layouts: 5.33 us -> 0 us
  Pallas kernels: 87.5 us -> 83.2 us
    pallas_call x1, Pallas kernels: 87.5 us -> 78.1 us  [shards(): pl.pallas_call(functools.partial(kernel, rows_all, cols_all), out_shape=(...]
    unnamed x11 -> x0, local copies, waits for them, and re-layouts: 5.33 us -> none
    pallas_call x0 -> x1, Pallas kernels: none -> 5.06 us  [shards(): pl.pallas_call(polar_kernel, out_shape=(*pots, jax.ShapeDtypeStruct((widt...]
where the time goes in v2:
time: 83.9 us; the launch traced here: 83.8 us
  Pallas kernels  83.2 us (99%)
    pallas_call x1, Pallas kernels, shards(): pl.pallas_call(functools.partial(kernel, rows_all, cols_all), out_shape=(...  78.1 us
    pallas_call x1, Pallas kernels, shards(): pl.pallas_call(polar_kernel, out_shape=(*pots, jax.ShapeDtypeStruct((widt...  5.06 us

profile of v2, /device:TPU:1, one launch (start us, length us, event | category | flops | bytes accessed | tf_op | source)
XLA Modules:
  0.0 83.8 jit_solution(2579265431447879779)
XLA Ops:
  0.6 78.1 %sinkhorn.1 = (f32[16,128]{1,0:T(8,128)}, f32[1,1024]{1,0:T(1,128)}, f32[8,16,128]{2,1,0:T(8,128)}) custom-call(bf16[2048,128]{1,0:T(8,128)(2,1)} %source_hbm.1, bf16[1024,128]{1,0:T(8,128)(2,1)} %target_hbm.1, f32[128,128]{1,0:T(8,128)} %map_hbm.1, f32[1,1024]{1,0:T(1,128)} %bitcast.3), custom_call_target="tpu_custom_call" | custom-call | tf_op jit(solution)/shard_map/sinkhorn/pallas_call | solution.py:411
  78.7 5.1 %polar.1 = (f32[16,128]{1,0:T(8,128)}, f32[1,1024]{1,0:T(1,128)}, f32[128,128]{1,0:T(8,128)}) custom-call(f32[8,16,128]{2,1,0:T(8,128)} %get-tuple-element.9.cross_ref, f32[16,128]{1,0:T(8,128)} %get-tuple-element.10.row_ref, f32[1,1024]{1,0:T(1,128)} %get-tuple-element.11.col_ref), custom_call_target="tpu_custom_call" | custom-call | tf_op jit(solution)/shard_map/polar/pallas_call | solution.py:444

commit v3 on v2

--- a/solution.py
+++ b/solution.py
@@ -17,6 +17,7 @@
 BF16 = jnp.bfloat16
 NX, NY, NZ, NC = 4, 4, 8, 2
 NSRC = NY * NC
+NPART = NSRC * NX
 L = 128
 
 
@@ -76,9 +77,8 @@
     row_z,
     row_x,
     col_s,
-    cross_s,
+    cross_p,
     cross_z,
-    cross_x,
     send_sem,
     recv_sem,
     load_sem,
@@ -107,8 +107,16 @@
     peers_z = [(me_s, me_x * NZ + lax.rem(me_z + k, NZ)) for k in (4, 3, 5, 2, 6, 1, 7)]
     peers_x = [(me_s, lax.rem(me_x + k, NX) * NZ + me_z) for k in (2, 1, 3)]
 
+    me_p = me_s * NX + me_x
+    peers_p = [
+        (lax.rem(me_s + b, NSRC), lax.rem(me_x + a, NX) * NZ + me_z)
+        for a in (2, 1, 3, 0)
+        for b in (4, 3, 5, 2, 6, 1, 7, 0)
+        if a or b
+    ]
+
     barrier = pltpu.get_barrier_semaphore()
-    everyone = peers_s + peers_z + peers_x
+    everyone = peers_z + peers_p
     for peer in everyone:
         pl.semaphore_signal(barrier, inc=1, device_id=peer, device_id_type=MESH)
 
@@ -189,8 +197,10 @@
         done.wait_recv()
         return combine([row_x[index, i] for i in range(NX)])
 
-    def col_reduce(index, combine):
+    def col_reduce(index, combine, meanwhile=None):
         done = send(3 * index + 2, col_s.at[index], me_s, peers_s)
+        if meanwhile is not None:
+            meanwhile()
         done.wait_recv()
         return combine([col_s[index, i] for i in range(NSRC)])
 
@@ -243,7 +253,6 @@
         for k in range(nk):
             e_val = jnp.exp2((e_f32[a, :, chunk(k)] + f_col) - peaks[k])
             e_f32[a, :, chunk(k)] = e_val
-            e_b16[a, :, chunk(k)] = e_val.astype(BF16)
             out.append(accs[k] + fold(e_val, jnp.add))
         return tuple(out)
 
@@ -252,7 +261,16 @@
     for k in range(nk):
         total = jnp.sum(sums[k], axis=0, keepdims=True)
         col_s[0, me_s, :, chunk(k)] = peaks[k] + jnp.log2(total)
-    col_lse = col_reduce(0, lse2)
+
+    def narrow():
+        def body(a, carry):
+            for k in range(nk):
+                e_b16[a, :, chunk(k)] = e_f32[a, :, chunk(k)].astype(BF16)
+            return carry
+
+        lax.fori_loop(0, nb, body, 0)
+
+    col_lse = col_reduce(0, lse2, narrow)
     g_first = warm2 - math.log2(cols_all) - col_lse
     local_weight = jnp.concatenate(
         [
@@ -332,36 +350,34 @@
     out = dot_nn(stacked, bary[...])
     cross[...] = (
         out[:width, :width] + out[:width, width:] + out[width:, :width] + out[width:, width:]
-    ).reshape(NSRC, width // NSRC, width)
+    ).reshape(NPART, width // NPART, width)
 
     phase = 3 * ROUNDS + 2
-    cross_s[me_s] = cross[me_s]
-    for peer in peers_s:
+    cross_p[me_p] = cross[me_p]
+    for peer in peers_p:
         pltpu.make_async_remote_copy(
-            src_ref=cross.at[peer[0]],
-            dst_ref=cross_s.at[me_s],
+            src_ref=cross.at[peer[0] * NX + peer[1] // NZ],
+            dst_ref=cross_p.at[me_p],
             send_sem=send_sem.at[phase],
             recv_sem=recv_sem.at[phase],
             device_id=peer,
             device_id_type=MESH,
         ).start()
-    others = cross_s.at[pl.ds(0, len(peers_s))]
+    others = cross_p.at[pl.ds(0, len(peers_p))]
     done = pltpu.make_async_remote_copy(
         src_ref=others,
         dst_ref=others,
         send_sem=send_sem.at[phase],
         recv_sem=recv_sem.at[phase],
-        device_id=peers_s[0],
+        device_id=peers_p[0],
         device_id_type=MESH,
     )
     pending.append(done)
     done.wait_recv()
-    cross_z[me_z] = total_of([cross_s[i] for i in range(NSRC)])
+    cross_z[me_z] = jnp.sum(cross_p[...], axis=0)
     send(phase + 1, cross_z, me_z, peers_z).wait_recv()
-    cross_x[me_x] = total_of([cross_z[i] for i in range(NZ)])
-    send(phase + 2, cross_x, me_x, peers_x).wait_recv()
-    cross_g[me_s] = total_of([cross_x[i] for i in range(NX)])
-    send(phase + 3, cross_g, me_s, peers_s).wait_recv()
+    cross_g[me_p] = jnp.sum(cross_z[...], axis=0)
+    send(phase + 2, cross_g, me_p, peers_p).wait_recv()
 
     for done in pending:
         done.wait_send()
@@ -393,7 +409,7 @@
         prod = dot_nn(pair_g, stack)
         return 1.5 * iterate - 0.5 * (prod[:, :width] + prod[:, width:])
 
-    result[...] = lax.fori_loop(0, NEWTON, newton, iterate)
+    result[...] = lax.fori_loop(0, NEWTON, newton, iterate, unroll=10)
     stores[2].start()
     for store in stores:
         store.wait()
@@ -404,14 +420,14 @@
     cols = target.shape[0]
     rows_all, cols_all = rows * lax.axis_size("src"), cols * lax.axis_size("tgt")
     nb, nk = rows // L, cols // L
-    phases = 3 * ROUNDS + 2 + 4
+    phases = 3 * ROUNDS + 2 + 3
     vmem = pltpu.VMEM
     pots = (jax.ShapeDtypeStruct((nb, L), F32), jax.ShapeDtypeStruct((1, cols), F32))
-    part_shape = (NSRC, width // NSRC, width)
+    part_shape = (NPART, width // NPART, width)
     row_pot, col_pot, cross = pl.pallas_call(
         functools.partial(kernel, rows_all, cols_all),
         out_shape=(*pots, jax.ShapeDtypeStruct(part_shape, F32)),
-        in_specs=[pl.BlockSpec(memory_space=pl.ANY)] * 4,
+        in_specs=[pl.BlockSpec(memory_space=pltpu.HBM)] * 4,
         out_specs=[pl.BlockSpec(memory_space=vmem)] * 3,
         scratch_shapes=[
             vmem((rows, width), BF16),
@@ -431,22 +447,27 @@
             vmem((ROUNDS, NSRC, 1, cols), F32),
             vmem(part_shape, F32),
             vmem((NZ, *part_shape[1:]), F32),
-            vmem((NX, *part_shape[1:]), F32),
             pltpu.SemaphoreType.DMA((phases,)),
             pltpu.SemaphoreType.DMA((phases,)),
             pltpu.SemaphoreType.DMA((4,)),
         ],
         compiler_params=pltpu.CompilerParams(
-            collective_id=0, has_side_effects=True, vmem_limit_bytes=60 << 20
+            collective_id=0, has_side_effects=True, vmem_limit_bytes=40 << 20
         ),
         name="sinkhorn",
-    )(source, target, start_map, warm_potential.reshape(1, cols))
+    )(
+        *(
+            pltpu.with_memory_space_constraint(arg, pltpu.HBM)
+            for arg in (source, target, start_map, warm_potential.reshape(1, cols))
+        )
+    )
     row_pot, col_pot, new_map = pl.pallas_call(
         polar_kernel,
         out_shape=(*pots, jax.ShapeDtypeStruct((width, width), F32)),
         in_specs=[pl.BlockSpec(memory_space=vmem)] * 3,
-        out_specs=[pl.BlockSpec(memory_space=pl.ANY)] * 3,
+        out_specs=[pl.BlockSpec(memory_space=pltpu.HBM)] * 3,
         scratch_shapes=[vmem((width, width), F32), pltpu.SemaphoreType.DMA((3,))],
+        compiler_params=pltpu.CompilerParams(vmem_limit_bytes=8 << 20),
         name="polar",
     )(cross, row_pot, col_pot)
     return row_pot.reshape(rows), col_pot.reshape(cols), new_map

time: 83.9 us -> 80.2 us (0.956)
  Pallas kernels: 83.2 us -> 79.5 us
    pallas_call x1, Pallas kernels: 78.1 us -> 75.5 us  [shards(): pl.pallas_call(functools.partial(kernel, rows_all, cols_all), out_shape=(...]
    pallas_call x1, Pallas kernels: 5.06 us -> 3.96 us  [shards(): pl.pallas_call(polar_kernel, out_shape=(*pots, jax.ShapeDtypeStruct((widt...]
where the time goes in v3:
time: 80.2 us; the launch traced here: 80.1 us
  Pallas kernels  79.5 us (99%)
    pallas_call x1, Pallas kernels, shards(): pl.pallas_call(functools.partial(kernel, rows_all, cols_all), out_shape=(...  75.5 us
    pallas_call x1, Pallas kernels, shards(): pl.pallas_call(polar_kernel, out_shape=(*pots, jax.ShapeDtypeStruct((widt...  3.96 us

profile of v3, /device:TPU:1, one launch (start us, length us, event | category | flops | bytes accessed | tf_op | source)
XLA Modules:
  0.0 80.1 jit_solution(7947822998256140212)
XLA Ops:
  0.6 75.5 %sinkhorn.1 = (f32[16,128]{1,0:T(8,128)S(1)}, f32[1,1024]{1,0:T(1,128)S(1)}, f32[32,4,128]{2,1,0:T(4,128)S(1)}) custom-call(bf16[2048,128]{1,0:T(8,128)(2,1)} %source_hbm.1, bf16[1024,128]{1,0:T(8,128)(2,1)} %target_hbm.1, f32[128,128]{1,0:T(8,128)} %map_hbm.1, f32[1,1024]{1,0:T(1,128)} %bitcast.3), custom_call_target="tpu_custom_call" | custom-call | tf_op jit(solution)/shard_map/sinkhorn/pallas_call | solution.py:427
  76.2 4.0 %polar.1 = (f32[16,128]{1,0:T(8,128)}, f32[1,1024]{1,0:T(1,128)}, f32[128,128]{1,0:T(8,128)}) custom-call(f32[32,4,128]{2,1,0:T(4,128)S(1)} %get-tuple-element.9.cross_ref, f32[16,128]{1,0:T(8,128)S(1)} %get-tuple-element.10.row_ref, f32[1,1024]{1,0:T(1,128)S(1)} %get-tuple-element.11.col_ref), custom_call_target="tpu_custom_call" | custom-call | tf_op jit(solution)/shard_map/polar/pallas_call | solution.py:464

commit v4 on v3

--- a/solution.py
+++ b/solution.py
@@ -18,6 +18,8 @@
 NX, NY, NZ, NC = 4, 4, 8, 2
 NSRC = NY * NC
 NPART = NSRC * NX
+HALVES = 2
+ROW_PHASES = 2 * HALVES * (ROUNDS + 1)
 L = 128
 
 
@@ -99,6 +101,7 @@
     rows, width = source_ref.shape
     cols = target_ref.shape[0]
     nb, nk = rows // L, cols // L
+    hb = nb // HALVES
     scale2 = 1.0 / (math.sqrt(width) * EPS) / LN2
     me_s = lax.axis_index("src")
     me_t = lax.axis_index("tgt")
@@ -157,18 +160,22 @@
     loads[3].wait()
     warm2 = warm_ref[...] * (1.0 / LN2)
     wide = 256
-    for k in range(cols // wide):
-        part = target_ref[pl.ds(k * wide, wide), :]
-        warm_part = warm2[:, k * wide : (k + 1) * wide]
-
-        def score_block(a, carry):
-            block = rot[pl.ds(pl.multiple_of(a * 512, 512), 512), :]
-            e_f32[pl.ds(a * 4, 4), :, pl.ds(k * wide, wide)] = (
-                dot_nt(block, part) * scale2 + warm_part
-            ).reshape(4, L, wide)
-            return carry
-
-        lax.fori_loop(0, rows // 512, score_block, 0, unroll=4)
+
+    def scores(half):
+        for k in range(cols // wide):
+            part = target_ref[pl.ds(k * wide, wide), :]
+            warm_part = warm2[:, k * wide : (k + 1) * wide]
+
+            def score_block(a, carry):
+                block = rot[pl.ds(pl.multiple_of(a * 512, 512), 512), :]
+                e_f32[pl.ds(a * 4, 4), :, pl.ds(k * wide, wide)] = (
+                    dot_nt(block, part) * scale2 + warm_part
+                ).reshape(4, L, wide)
+                return carry
+
+            first_block = half * hb * L // 512
+            last_block = (half + 1) * hb * L // 512
+            lax.fori_loop(first_block, last_block, score_block, 0, unroll=True)
 
     def first_row(a, acc):
         peak = e_f32[a, :, chunk(0)]
@@ -181,34 +188,44 @@
         total = jnp.sum(total, axis=1, keepdims=True)
         return jnp.where(lane == a, peak + jnp.log2(total), acc)
 
-    first = lax.fori_loop(0, nb, first_row, zero_tile, unroll=4)
-    pl.semaphore_wait(barrier, len(everyone))
-
-    def row_reduce(index, tile, combine, meanwhile=None, meanwhile2=None):
-        row_z[index, me_z] = tile.T[:nb]
-        done = send(3 * index, row_z.at[index], me_z, peers_z)
-        if meanwhile is not None:
-            meanwhile()
-        done.wait_recv()
-        row_x[index, me_x] = combine([row_z[index, i] for i in range(NZ)])
-        done = send(3 * index + 1, row_x.at[index], me_x, peers_x)
-        if meanwhile2 is not None:
-            meanwhile2()
-        done.wait_recv()
-        return combine([row_x[index, i] for i in range(NX)])
+    def row_send(index, half, tile):
+        row_z[index, half, me_z] = tile.T[half * hb : (half + 1) * hb]
+        phase = 2 * (index * HALVES + half)
+        return send(phase, row_z.at[index, half], me_z, peers_z)
+
+    def row_receive(index, done, combine, consume):
+        later = []
+        for half in range(HALVES):
+            done[half].wait_recv()
+            row_x[index, half, me_x] = combine([row_z[index, half, i] for i in range(NZ)])
+            phase = 2 * (index * HALVES + half) + 1
+            later.append(send(phase, row_x.at[index, half], me_x, peers_x))
+        for half in range(HALVES):
+            later[half].wait_recv()
+            consume(half, combine([row_x[index, half, i] for i in range(NX)]))
+
+    sent = []
+    for half in range(HALVES):
+        scores(half)
+        tile = lax.fori_loop(half * hb, (half + 1) * hb, first_row, zero_tile, unroll=4)
+        if half == 0:
+            pl.semaphore_wait(barrier, len(everyone))
+        sent.append(row_send(0, half, tile))
 
     def col_reduce(index, combine, meanwhile=None):
-        done = send(3 * index + 2, col_s.at[index], me_s, peers_s)
+        done = send(ROW_PHASES + index, col_s.at[index], me_s, peers_s)
         if meanwhile is not None:
             meanwhile()
         done.wait_recv()
         return combine([col_s[index, i] for i in range(NSRC)])
 
-    def spread(value):
-        u_t[...] = jnp.concatenate([value, jnp.zeros((L - nb, L), F32)], axis=0).T
-
-    def column_of(a):
-        return jnp.sum(jnp.where(lane == a, u_t[...], 0.0), axis=1, keepdims=True)
+    def spread(half, value):
+        u_t[half] = jnp.concatenate([value, jnp.zeros((L - hb, L), F32)], axis=0).T
+
+    def column_of(half, a):
+        return jnp.sum(
+            jnp.where(lane == a - half * hb, u_t[half], 0.0), axis=1, keepdims=True
+        )
 
     def fold(tile, op):
         parts = [tile[8 * i : 8 * i + 8] for i in range(L // 8)]
@@ -231,24 +248,29 @@
 
         lax.fori_loop(0, nk, one_target, 0)
 
-    row_lse = row_reduce(0, first, lse2, transposes)
-    f_first = -math.log2(rows_all) - row_lse
-    spread(f_first)
-
-    def first_col_peak(a, accs):
-        f_col = column_of(a)
-        return tuple(
-            jnp.maximum(accs[k], fold(e_f32[a, :, chunk(k)] + f_col, jnp.maximum))
-            for k in range(nk)
-        )
-
-    peaks = lax.fori_loop(
-        0, nb, first_col_peak, tuple(jnp.full((8, L), -jnp.inf, F32) for _ in range(nk)), unroll=8
-    )
+    transposes()
+    f_first = [None] * HALVES
+    peaks = tuple(jnp.full((8, L), -jnp.inf, F32) for _ in range(nk))
+
+    def first_cols(half, row_lse):
+        nonlocal peaks
+        f_first[half] = -math.log2(rows_all) - row_lse
+        spread(half, f_first[half])
+
+        def body(a, accs):
+            f_col = column_of(half, a)
+            return tuple(
+                jnp.maximum(accs[k], fold(e_f32[a, :, chunk(k)] + f_col, jnp.maximum))
+                for k in range(nk)
+            )
+
+        peaks = lax.fori_loop(half * hb, (half + 1) * hb, body, peaks, unroll=8)
+
+    row_receive(0, sent, lse2, first_cols)
     peaks = [jnp.max(p, axis=0, keepdims=True) for p in peaks]
 
-    def first_col_sum(a, accs):
-        f_col = column_of(a)
+    def first_col_sum(half, a, accs):
+        f_col = column_of(half, a)
         out = []
         for k in range(nk):
             e_val = jnp.exp2((e_f32[a, :, chunk(k)] + f_col) - peaks[k])
@@ -257,7 +279,15 @@
         return tuple(out)
 
     zeros = tuple(jnp.zeros((8, L), F32) for _ in range(nk))
-    sums = lax.fori_loop(0, nb, first_col_sum, zeros, unroll=4)
+    sums = zeros
+    for half in range(HALVES):
+        sums = lax.fori_loop(
+            half * hb,
+            (half + 1) * hb,
+            functools.partial(first_col_sum, half),
+            sums,
+            unroll=4,
+        )
     for k in range(nk):
         total = jnp.sum(sums[k], axis=0, keepdims=True)
         col_s[0, me_s, :, chunk(k)] = peaks[k] + jnp.log2(total)
@@ -280,7 +310,7 @@
         axis=1,
     )
 
-    def row_pass(weight):
+    def row_pass(index, weight):
         weights = [weight[:, k * L : (k + 1) * L] for k in range(nk)]
 
         def body(a, acc):
@@ -290,16 +320,28 @@
             total = jnp.sum(total, axis=1, keepdims=True)
             return jnp.where(lane == a, total, acc)
 
-        return lax.fori_loop(0, nb, body, zero_tile, unroll=16)
-
-    def col_pass(index):
-        def body(a, accs):
-            u_col = column_of(a)
-            return tuple(
-                accs[k] + fold(e_f32[a, :, chunk(k)] * u_col, jnp.add) for k in range(nk)
-            )
-
-        sums = lax.fori_loop(0, nb, body, zeros, unroll=16)
+        sent = []
+        for half in range(HALVES):
+            tile = lax.fori_loop(half * hb, (half + 1) * hb, body, zero_tile, unroll=hb)
+            sent.append(row_send(index, half, tile))
+        return sent
+
+    def col_pass(index, sent):
+        sums = zeros
+
+        def consume(half, mass):
+            nonlocal sums
+            spread(half, 1.0 / (mass * rows_all))
+
+            def body(a, accs):
+                u_col = column_of(half, a)
+                return tuple(
+                    accs[k] + fold(e_f32[a, :, chunk(k)] * u_col, jnp.add) for k in range(nk)
+                )
+
+            sums = lax.fori_loop(half * hb, (half + 1) * hb, body, sums, unroll=hb)
+
+        row_receive(index, sent, total_of, consume)
         for k in range(nk):
             total = jnp.sum(sums[k], axis=0, keepdims=True)
             col_s[index, me_s, :, chunk(k)] = total * local_weight[:, k * L : (k + 1) * L]
@@ -307,9 +349,7 @@
     weight = local_weight
     v_val = None
     for index in range(1, ROUNDS):
-        mass = row_reduce(index, row_pass(weight), total_of)
-        spread(1.0 / (mass * rows_all))
-        col_pass(index)
+        col_pass(index, row_pass(index, weight))
         v_val = 1.0 / (col_reduce(index, total_of) * cols_all)
         weight = local_weight * v_val
 
@@ -335,11 +375,19 @@
 
         lax.fori_loop(0, nb // 4, body, 0, unroll=2)
 
-    mass = row_reduce(ROUNDS, row_pass(weight), total_of, barycentric)
-    row_out[...] = (EPS * LN2) * (f_first - math.log2(rows_all) - jnp.log2(mass))
-    inverse = 1.0 / mass
-
-    pieces = [split(src_t[a] * inverse[a : a + 1, :]) for a in range(nb)]
+    sent = row_pass(ROUNDS, weight)
+    barycentric()
+    inverse = []
+
+    def last_rows(half, mass):
+        row_out[pl.ds(half * hb, hb), :] = (EPS * LN2) * (
+            f_first[half] - math.log2(rows_all) - jnp.log2(mass)
+        )
+        recip = 1.0 / mass
+        inverse.extend(recip[i : i + 1, :] for i in range(hb))
+
+    row_receive(ROUNDS, sent, total_of, last_rows)
+    pieces = [split(src_t[a] * inverse[a]) for a in range(nb)]
     stacked = jnp.concatenate(
         [
             jnp.concatenate([p[0] for p in pieces], axis=1),
@@ -352,7 +400,7 @@
         out[:width, :width] + out[:width, width:] + out[width:, :width] + out[width:, width:]
     ).reshape(NPART, width // NPART, width)
 
-    phase = 3 * ROUNDS + 2
+    phase = ROW_PHASES + ROUNDS
     cross_p[me_p] = cross[me_p]
     for peer in peers_p:
         pltpu.make_async_remote_copy(
@@ -420,7 +468,7 @@
     cols = target.shape[0]
     rows_all, cols_all = rows * lax.axis_size("src"), cols * lax.axis_size("tgt")
     nb, nk = rows // L, cols // L
-    phases = 3 * ROUNDS + 2 + 3
+    phases = ROW_PHASES + ROUNDS + 3
     vmem = pltpu.VMEM
     pots = (jax.ShapeDtypeStruct((nb, L), F32), jax.ShapeDtypeStruct((1, cols), F32))
     part_shape = (NPART, width // NPART, width)
@@ -440,10 +488,10 @@
             vmem((nb, width, L), F32),
             vmem((nk, width, L), F32),
             vmem((rows, 2 * width), BF16),
-            vmem((L, L), F32),
+            vmem((HALVES, L, L), F32),
             vmem(part_shape, F32),
-            vmem((ROUNDS + 1, NZ, nb, L), F32),
-            vmem((ROUNDS + 1, NX, nb, L), F32),
+            vmem((ROUNDS + 1, HALVES, NZ, nb // HALVES, L), F32),
+            vmem((ROUNDS + 1, HALVES, NX, nb // HALVES, L), F32),
             vmem((ROUNDS, NSRC, 1, cols), F32),
             vmem(part_shape, F32),
             vmem((NZ, *part_shape[1:]), F32),

time: 80.2 us -> 79.6 us (level)
  no operation moved by 1% of the time
where the time goes in v4:
time: 79.6 us; the launch traced here: 79.5 us
  Pallas kernels  78.8 us (99%)
    pallas_call x1, Pallas kernels, shards(): pl.pallas_call(functools.partial(kernel, rows_all, cols_all), out_shape=(...  74.9 us
    pallas_call x1, Pallas kernels, shards(): pl.pallas_call(polar_kernel, out_shape=(*pots, jax.ShapeDtypeStruct((widt...  3.96 us

profile of v4, /device:TPU:1, one launch (start us, length us, event | category | flops | bytes accessed | tf_op | source)
XLA Modules:
  0.0 79.5 jit_solution(2143534371733609850)
XLA Ops:
  0.6 74.9 %sinkhorn.1 = (f32[16,128]{1,0:T(8,128)S(1)}, f32[1,1024]{1,0:T(1,128)S(1)}, f32[32,4,128]{2,1,0:T(4,128)S(1)}) custom-call(bf16[2048,128]{1,0:T(8,128)(2,1)} %source_hbm.1, bf16[1024,128]{1,0:T(8,128)(2,1)} %target_hbm.1, f32[128,128]{1,0:T(8,128)} %map_hbm.1, f32[1,1024]{1,0:T(1,128)} %bitcast.3), custom_call_target="tpu_custom_call" | custom-call | tf_op jit(solution)/shard_map/sinkhorn/pallas_call | solution.py:475
  75.5 4.0 %polar.1 = (f32[16,128]{1,0:T(8,128)}, f32[1,1024]{1,0:T(1,128)}, f32[128,128]{1,0:T(8,128)}) custom-call(f32[32,4,128]{2,1,0:T(4,128)S(1)} %get-tuple-element.9.cross_ref, f32[16,128]{1,0:T(8,128)S(1)} %get-tuple-element.10.row_ref, f32[1,1024]{1,0:T(1,128)S(1)} %get-tuple-element.11.col_ref), custom_call_target="tpu_custom_call" | custom-call | tf_op jit(solution)/shard_map/polar/pallas_call | solution.py:512

commit v5 on v4

--- a/solution.py
+++ b/solution.py
@@ -119,7 +119,7 @@
     ]
 
     barrier = pltpu.get_barrier_semaphore()
-    everyone = peers_z + peers_p
+    everyone = peers_z + peers_s + peers_x
     for peer in everyone:
         pl.semaphore_signal(barrier, inc=1, device_id=peer, device_id_type=MESH)
 

time: 79.6 us -> 79.2 us (level)
  no operation moved by 1% of the time
where the time goes in v5:
time: 79.2 us; the launch traced here: 79.1 us
  Pallas kernels  78.4 us (99%)
    pallas_call x1, Pallas kernels, shards(): pl.pallas_call(functools.partial(kernel, rows_all, cols_all), out_shape=(...  74.5 us
    pallas_call x1, Pallas kernels, shards(): pl.pallas_call(polar_kernel, out_shape=(*pots, jax.ShapeDtypeStruct((widt...  3.96 us

profile of v5, /device:TPU:1, one launch (start us, length us, event | category | flops | bytes accessed | tf_op | source)
XLA Modules:
  0.0 79.1 jit_solution(16356885054192709136)
XLA Ops:
  0.6 74.5 %sinkhorn.1 = (f32[16,128]{1,0:T(8,128)S(1)}, f32[1,1024]{1,0:T(1,128)S(1)}, f32[32,4,128]{2,1,0:T(4,128)S(1)}) custom-call(bf16[2048,128]{1,0:T(8,128)(2,1)} %source_hbm.1, bf16[1024,128]{1,0:T(8,128)(2,1)} %target_hbm.1, f32[128,128]{1,0:T(8,128)} %map_hbm.1, f32[1,1024]{1,0:T(1,128)} %bitcast.3), custom_call_target="tpu_custom_call" | custom-call | tf_op jit(solution)/shard_map/sinkhorn/pallas_call | solution.py:475
  75.1 4.0 %polar.1 = (f32[16,128]{1,0:T(8,128)}, f32[1,1024]{1,0:T(1,128)}, f32[128,128]{1,0:T(8,128)}) custom-call(f32[32,4,128]{2,1,0:T(4,128)S(1)} %get-tuple-element.9.cross_ref, f32[16,128]{1,0:T(8,128)S(1)} %get-tuple-element.10.row_ref, f32[1,1024]{1,0:T(1,128)S(1)} %get-tuple-element.11.col_ref), custom_call_target="tpu_custom_call" | custom-call | tf_op jit(solution)/shard_map/polar/pallas_call | solution.py:512

commit v6 on v5

--- a/solution.py
+++ b/solution.py
@@ -378,11 +378,10 @@
     sent = row_pass(ROUNDS, weight)
     barycentric()
     inverse = []
+    masses = []
 
     def last_rows(half, mass):
-        row_out[pl.ds(half * hb, hb), :] = (EPS * LN2) * (
-            f_first[half] - math.log2(rows_all) - jnp.log2(mass)
-        )
+        masses.append(mass)
         recip = 1.0 / mass
         inverse.extend(recip[i : i + 1, :] for i in range(hb))
 
@@ -401,7 +400,6 @@
     ).reshape(NPART, width // NPART, width)
 
     phase = ROW_PHASES + ROUNDS
-    cross_p[me_p] = cross[me_p]
     for peer in peers_p:
         pltpu.make_async_remote_copy(
             src_ref=cross.at[peer[0] * NX + peer[1] // NZ],
@@ -411,6 +409,11 @@
             device_id=peer,
             device_id_type=MESH,
         ).start()
+    cross_p[me_p] = cross[me_p]
+    for half in range(HALVES):
+        row_out[pl.ds(half * hb, hb), :] = (EPS * LN2) * (
+            f_first[half] - math.log2(rows_all) - jnp.log2(masses[half])
+        )
     others = cross_p.at[pl.ds(0, len(peers_p))]
     done = pltpu.make_async_remote_copy(
         src_ref=others,

time: 79.2 us -> 79.2 us (level)
  no operation moved by 1% of the time
where the time goes in v6:
time: 79.2 us; the launch traced here: 79.1 us
  Pallas kernels  78.4 us (99%)
    pallas_call x1, Pallas kernels, shards(): pl.pallas_call(functools.partial(kernel, rows_all, cols_all), out_shape=(...  74.5 us
    pallas_call x1, Pallas kernels, shards(): pl.pallas_call(polar_kernel, out_shape=(*pots, jax.ShapeDtypeStruct((widt...  3.96 us

profile of v6, /device:TPU:1, one launch (start us, length us, event | category | flops | bytes accessed | tf_op | source)
XLA Modules:
  0.0 79.1 jit_solution(12410069593845044473)
XLA Ops:
  0.6 74.5 %sinkhorn.1 = (f32[16,128]{1,0:T(8,128)S(1)}, f32[1,1024]{1,0:T(1,128)S(1)}, f32[32,4,128]{2,1,0:T(4,128)S(1)}) custom-call(bf16[2048,128]{1,0:T(8,128)(2,1)} %source_hbm.1, bf16[1024,128]{1,0:T(8,128)(2,1)} %target_hbm.1, f32[128,128]{1,0:T(8,128)} %map_hbm.1, f32[1,1024]{1,0:T(1,128)} %bitcast.3), custom_call_target="tpu_custom_call" | custom-call | tf_op jit(solution)/shard_map/sinkhorn/pallas_call | solution.py:478
  75.1 4.0 %polar.1 = (f32[16,128]{1,0:T(8,128)}, f32[1,1024]{1,0:T(1,128)}, f32[128,128]{1,0:T(8,128)}) custom-call(f32[32,4,128]{2,1,0:T(4,128)S(1)} %get-tuple-element.9.cross_ref, f32[16,128]{1,0:T(8,128)S(1)} %get-tuple-element.10.row_ref, f32[1,1024]{1,0:T(1,128)S(1)} %get-tuple-element.11.col_ref), custom_call_target="tpu_custom_call" | custom-call | tf_op jit(solution)/shard_map/polar/pallas_call | solution.py:515
